TPU v7x, 512 devices: a whole 4x8x8 slice. The times are simulated.
512 devices in a mesh: dp: 8 (over x, core), ctx: 64 (over z, y).
Axes of the slice: x: 4, y: 8, z: 8, core: 2. Of those that a mesh axis runs over, the one named last changes fastest.
Arguments:
- queries: bfloat16 [65536, 32, 128], P(('dp', 'ctx')), parts along dimension 0, may hold values from -10 to 10
- keys: bfloat16 [65536, 4, 128], P(('dp', 'ctx')), parts along dimension 0, may hold values from -10 to 10
- values: bfloat16 [65536, 4, 128], P(('dp', 'ctx')), parts along dimension 0, may hold values from -6 to 6
- segment: int32 [65536], P(('dp', 'ctx')), parts along dimension 0, may hold values from 0 to 31, never falling along the last dimension, each value on 1 to 768 neighbouring positions
- grad_out: bfloat16 [65536, 32, 128], P(('dp', 'ctx')), parts along dimension 0, may hold values from -6 to 6
Outputs:
- attended: bfloat16 [65536, 32, 128], P(('dp', 'ctx')), parts along dimension 0
- grad_queries: bfloat16 [65536, 32, 128], P(('dp', 'ctx')), parts along dimension 0
- grad_keys: bfloat16 [65536, 4, 128], P(('dp', 'ctx')), parts along dimension 0
- grad_values: bfloat16 [65536, 4, 128], P(('dp', 'ctx')), parts along dimension 0
There are 8 independent parts, one for each index of `dp`. A program takes and returns all parts, laid end to end along the dimension named above; each array names one. Nothing has to cross between parts.
Inputs may be any that keep to these rules, and one draw needn't show every extreme that they name: `segment`: documents are runs of consecutive positions numbered in order; each holds 1 to 768 positions and one holds exactly 768.
All inputs are finite; a program needn't handle non-finite values.
Results may differ from a plain program's by a relative error of at most 0.012.
The roundings to bfloat16 on the way count: a program that leaves them out, or rounds other values in their place, can miss the bound.
Values may be sent and summed in bfloat16 or wider, within the bound.
No kernel may reach another device: no remote copies, remote signals or barrier semaphores. Data moves between devices by JAX's collectives and lax.ppermute only.
A program may use at most 128 MiB of HBM per device.

v0:
```python
import jax
import jax.numpy as jnp
from jax import lax
from jax.sharding import PartitionSpec as P

SPAN = 6


negative_fill = -1e30


def prefix(part, axis, combine, identity):
    place = lax.axis_index(axis)
    gathered = jax.tree.map(lambda a: lax.all_gather(a, axis), part)
    state = jax.tree.map(lambda a, e: jnp.zeros_like(a) + jnp.asarray(e, a.dtype), part, identity)

    def one(turn, state):
        return combine(
            state, jax.tree.map(lambda a: lax.dynamic_index_in_dim(a, turn, 0, False), gathered)
        )

    return lax.fori_loop(0, place, one, state)


def from_behind(value, axis, steps):
    count = lax.axis_size(axis)
    initial, last = (max(0, -steps), min(count, count - steps))
    return lax.ppermute(value, axis, [(source, source + steps) for source in range(initial, last)])


def for_sending(shard):

    def short(part):
        return part.astype(jnp.bfloat16) if part.dtype == jnp.float32 else part

    return jax.tree.map(short, shard)


def join_runs(earlier, later):
    early_seg, early_start = earlier
    late_seg, late_start = later
    absent = late_seg < 0
    joined = late_seg == early_seg
    seg_out = jnp.where(absent, early_seg, late_seg)
    start_out = jnp.where(
        absent, early_start, jnp.where(joined, jnp.minimum(early_start, late_start), late_start)
    )
    return (seg_out, start_out)


def shards(queries, keys, values, segment, grad_out):
    shard_rows, head_count, head_dim = queries.shape
    group_count = keys.shape[1]
    per_group = head_count // group_count
    softmax_scale = head_dim ** (-0.5)
    device = lax.axis_index("ctx")
    offsets = jnp.arange(shard_rows, dtype=jnp.int32)
    query_pos = device * shard_rows + offsets
    starts_here = jnp.concatenate([jnp.ones((1,), jnp.bool_), segment[1:] != segment[:-1]])
    own_start = lax.cummax(jnp.where(starts_here, query_pos, 0), axis=0)
    identity = (jnp.full((1,), -1, jnp.int32), jnp.full((1,), 2**30, jnp.int32))
    prev_seg, prev_start = prefix((segment[-1:], own_start[-1:]), "ctx", join_runs, identity)
    doc_start = jnp.where(segment == prev_seg, jnp.minimum(prev_start, own_start), own_start)
    pieces = [None] * (SPAN + 1)
    pieces[SPAN] = (keys, values)
    moving = (keys, values)
    for hop_index in range(1, SPAN + 1):
        moving = from_behind((moving[0], moving[1]), "ctx", 1)
        pieces[SPAN - hop_index] = moving
    key_window = jnp.concatenate([piece[0] for piece in pieces], 0)
    value_window = jnp.concatenate([piece[1] for piece in pieces], 0)
    window = key_window.shape[0]
    rows_here = device * shard_rows + offsets
    keys_here = (device - SPAN) * shard_rows + jnp.arange(window, dtype=jnp.int32)
    visible = (keys_here[None, :] <= rows_here[:, None]) & (
        keys_here[None, :] >= doc_start[:, None]
    )

    def pair_products(query_head, grad_head, key_part, value_part):
        return (
            jnp.einsum("tgd,wd->tgw", query_head, key_part, preferred_element_type=jnp.float32),
            jnp.einsum("tgd,wd->tgw", grad_head, value_part, preferred_element_type=jnp.float32),
        )

    def grad_products(dscore_part, probs_part, query_head, grad_head):
        return (
            jnp.einsum("tgw,tgd->wd", dscore_part, query_head, preferred_element_type=jnp.float32),
            jnp.einsum("tgw,tgd->wd", probs_part, grad_head, preferred_element_type=jnp.float32),
        )

    def head_terms(inputs, seen):
        query_head, key_head, value_head, grad_head = inputs
        scores, dprobs = pair_products(query_head, grad_head, key_head, value_head)
        scores = jnp.where(seen[:, None, :], scores * softmax_scale, negative_fill)
        row_max = jnp.max(scores, axis=-1, keepdims=True)
        shifted_exp = jnp.exp(scores - row_max)
        probs_full = shifted_exp / jnp.sum(shifted_exp, axis=-1, keepdims=True)
        probs_half = probs_full.astype(jnp.bfloat16)
        attended = jnp.einsum(
            "tgw,wd->tgd", probs_half, value_head, preferred_element_type=jnp.float32
        ).astype(jnp.bfloat16)
        row_delta = jnp.sum(grad_head.astype(jnp.float32) * attended.astype(jnp.float32), axis=-1)
        dscore = (probs_full * (dprobs - row_delta[..., None])).astype(jnp.bfloat16)
        grad_query = (
            jnp.einsum("tgw,wd->tgd", dscore, key_head, preferred_element_type=jnp.float32)
            * softmax_scale
        ).astype(jnp.bfloat16)
        grad_key, grad_value = grad_products(dscore, probs_half, query_head, grad_head)
        return (attended, grad_query, grad_key * softmax_scale, grad_value)

    query_heads = jnp.transpose(
        queries.reshape(shard_rows, group_count, per_group, head_dim), (1, 0, 2, 3)
    )
    grad_heads = jnp.transpose(
        grad_out.reshape(shard_rows, group_count, per_group, head_dim), (1, 0, 2, 3)
    )
    key_heads = jnp.transpose(key_window, (1, 0, 2))
    value_heads = jnp.transpose(value_window, (1, 0, 2))
    attended, grad_query, grad_key, grad_value = lax.map(
        lambda member: head_terms(member, visible),
        (query_heads, key_heads, value_heads, grad_heads),
    )
    attended = jnp.transpose(attended, (1, 0, 2, 3)).reshape(shard_rows, head_count, head_dim)
    grad_queries = jnp.transpose(grad_query, (1, 0, 2, 3)).reshape(shard_rows, head_count, head_dim)
    key_parts = jnp.transpose(
        grad_key.reshape(group_count, SPAN + 1, shard_rows, head_dim), (1, 2, 0, 3)
    )
    value_parts = jnp.transpose(
        grad_value.reshape(group_count, SPAN + 1, shard_rows, head_dim), (1, 2, 0, 3)
    )
    running = (key_parts[0], value_parts[0])
    for hop_index in range(1, SPAN + 1):
        running = from_behind((for_sending(running[0]), for_sending(running[1])), "ctx", -1)
        running = (running[0] + key_parts[hop_index], running[1] + value_parts[hop_index])
    key_total, value_total = running
    return (
        attended,
        grad_queries,
        key_total.astype(jnp.bfloat16),
        value_total.astype(jnp.bfloat16),
    )


def solution(mesh):
    return jax.shard_map(
        shards,
        mesh=mesh,
        in_specs=(
            P(("dp", "ctx"), None, None),
            P(("dp", "ctx"), None, None),
            P(("dp", "ctx"), None, None),
            P(("dp", "ctx")),
            P(("dp", "ctx"), None, None),
        ),
        out_specs=(
            P(("dp", "ctx"), None, None),
            P(("dp", "ctx"), None, None),
            P(("dp", "ctx"), None, None),
            P(("dp", "ctx"), None, None),
        ),
        check_vma=False,
    )
```

profile of v0, /device:TPU:478, one launch (start us, length us, event | category | flops | bytes accessed | tf_op | source)
XLA Modules:
  0.0 553.6 jit_solution(1335436241508754596)
XLA Ops:
  1.8 4.7 collective-permute-start.6
  7.4 2.6 collective-permute-start
  10.0 4.8 collective-permute-start.7
  14.8 3.2 collective-permute-start.1
  18.1 5.5 %collective-permute-start.8 = (bf16[128,4,128]{0,2,1:T(8,128)(2,1)S(1)}, bf16[128,4,128]{0,2,1:T(8,128)(2,1)S(1)}, u32[]{:S(2)}, u32[]{:S(2)}) collective-permute-start(bf16[128,4,128]{0,2,1:T(8,128)(2,1)S(1)} %collective-permute-done.7), channel_id=1, source_target_pairs={{0,1},{1,2},{2,3},{3,4},{4,5},{5,6},{6,7},{7,8},{8,9},{9,10},{10,1... | collective-permute-start | bytes 393224 | tf_op jit(solution)/shard_map/ppermute | solution.py:28
  23.6 2.5 collective-permute-start.2
  27.0 5.6 %collective-permute-start.9 = (bf16[128,4,128]{0,2,1:T(8,128)(2,1)S(1)}, bf16[128,4,128]{0,2,1:T(8,128)(2,1)S(1)}, u32[]{:S(2)}, u32[]{:S(2)}) collective-permute-start(bf16[128,4,128]{0,2,1:T(8,128)(2,1)S(1)} %collective-permute-done.8), channel_id=1, source_target_pairs={{0,1},{1,2},{2,3},{3,4},{4,5},{5,6},{6,7},{7,8},{8,9},{9,10},{10,1... | collective-permute-start | bytes 393224 | tf_op jit(solution)/shard_map/ppermute | solution.py:28
  33.4 1.9 collective-permute-start.3
  35.3 5.4 collective-permute-start.10
  45.9 19.6 %all-reduce.2 = (s32[64]{0:T(128)S(1)}, s32[64]{0:T(128)S(1)}) all-reduce(s32[64]{0:T(128)S(1)} %slice_dynamic-update-slice_fusion, s32[64]{0:T(128)S(1)} %bitcast_dynamic-update-slice_fusion.1), channel_id=2, replica_groups=mesh['dp'=8,'ctx'=64] {'ctx'}, use_global_device_ids=true, to_apply=%add | all-reduce | flops 128 | bytes 1024
  65.4 227.8 %while.29 = (s32[]{:T(128)}, s32[1]{0:T(128)}, s32[1]{0:T(128)}, s32[]{:T(128)}, s32[64,1]{0,1:T(1,128)S(1)}, /*index=5*/s32[64,1]{0,1:T(1,128)S(1)}, s32[]{:T(128)}, s32[]{:T(128)}, s32[]{:T(128)}, s32[1]{0:T(128)}) while((s32[]{:T(128)}, s32[1]{0:T(128)}, s32[1]{0:T(128)}, s32[]{:T(128)}, s32[64,1]{0,1:T(1,128)S(1)}, ...), condition=%wide.region_2.3_spmd, body=%wide.region_1.2_spmd.sunk | while | flops 11 | bytes 232 | solution.py:22
  293.3 7.1 %collective-permute-start.4 = (bf16[128,4,128]{2,0,1:T(8,128)(2,1)}, bf16[128,4,128]{2,0,1:T(8,128)(2,1)}, u32[]{:S(2)}, u32[]{:S(2)}) collective-permute-start(bf16[128,4,128]{2,0,1:T(8,128)(2,1)} %collective-permute-done.3), channel_id=1, source_target_pairs={{0,1},{1,2},{2,3},{3,4},{4,5},{5,6},{6,7},{7,8},{8,9},{9,10},{10,1... | collective-permute-start | bytes 393224 | tf_op jit(solution)/shard_map/ppermute | solution.py:28
  300.4 5.1 collective-permute-start.11
  308.9 10.8 %collective-permute-start.5 = (bf16[128,4,128]{2,0,1:T(8,128)(2,1)}, bf16[128,4,128]{2,0,1:T(8,128)(2,1)S(1)}, u32[]{:S(2)}, u32[]{:S(2)}) collective-permute-start(bf16[128,4,128]{2,0,1:T(8,128)(2,1)} %collective-permute-done.4), channel_id=1, source_target_pairs={{0,1},{1,2},{2,3},{3,4},{4,5},{5,6},{6,7},{7,8},{8,9},{9,10},{10,1... | collective-permute-start | bytes 393224 | tf_op jit(solution)/shard_map/ppermute | solution.py:28
  331.9 162.5 %while.30 = (s32[]{:T(128)}, bf16[4,128,8,128]{1,3,2,0:T(8,128)(2,1)}, bf16[4,128,8,128]{3,1,2,0:T(8,128)(2,1)}, f32[4,896,128]{2,0,1:T(4,128)}, f32[4,896,128]{...) while((s32[]{:T(128)}, ...), condition=%wide.region_7.8_spmd.clone, body=%wide.region_3.7_spmd.clone.sunk | while | flops 1419837312 | bytes 42988220 | solution.py:119
  332.1 4.2 fusion.123
  336.3 2.4 fusion.124
  339.4 2.7 bitcast_dynamic-update-slice_fusion.3
  342.2 1.8 multiply_convert_fusion.2
  344.7 2.3 fusion.125
  347.0 12.8 %dynamic_update_slice.26 = f32[4,896,128]{2,0,1:T(4,128)} dynamic-update-slice(f32[4,896,128]{2,0,1:T(4,128)} %get-tuple-element.368, f32[1,896,128]{2,0,1:T(1,128)S(1)} %bitcast.214, s32[]{:T(128)S(6)} %copy.88, s32[]{:T(128)} %constant.54.clone.1..sunk.1, s32[]{:T(128)} %constant.54.clone.1..sunk.1) | dynamic-update-slice | bytes 917508 | tf_op jit(solution)/shard_map/while/body/jit(dynamic_update_index_in_dim)/dynamic_update_slice | solution.py:119
  359.8 12.8 %dynamic_update_slice.27 = f32[4,896,128]{2,0,1:T(4,128)} dynamic-update-slice(f32[4,896,128]{2,0,1:T(4,128)} %get-tuple-element.369, f32[1,896,128]{2,0,1:T(1,128)S(1)} %bitcast.213, s32[]{:T(128)S(6)} %copy.88, s32[]{:T(128)} %constant.54.clone.1..sunk.1, s32[]{:T(128)} %constant.54.clone.1..sunk.1) | dynamic-update-slice | bytes 917508 | tf_op jit(solution)/shard_map/while/body/jit(dynamic_update_index_in_dim)/dynamic_update_slice | solution.py:119
  372.7 4.2 fusion.123
  376.9 2.4 fusion.124
  380.0 2.7 bitcast_dynamic-update-slice_fusion.3
  385.3 2.3 fusion.125
  387.6 12.8 %dynamic_update_slice.26 = f32[4,896,128]{2,0,1:T(4,128)} dynamic-update-slice(f32[4,896,128]{2,0,1:T(4,128)} %get-tuple-element.368, f32[1,896,128]{2,0,1:T(1,128)S(1)} %bitcast.214, s32[]{:T(128)S(6)} %copy.88, s32[]{:T(128)} %constant.54.clone.1..sunk.1, s32[]{:T(128)} %constant.54.clone.1..sunk.1) | dynamic-update-slice | bytes 917508 | tf_op jit(solution)/shard_map/while/body/jit(dynamic_update_index_in_dim)/dynamic_update_slice | solution.py:119
  400.4 12.8 %dynamic_update_slice.27 = f32[4,896,128]{2,0,1:T(4,128)} dynamic-update-slice(f32[4,896,128]{2,0,1:T(4,128)} %get-tuple-element.369, f32[1,896,128]{2,0,1:T(1,128)S(1)} %bitcast.213, s32[]{:T(128)S(6)} %copy.88, s32[]{:T(128)} %constant.54.clone.1..sunk.1, s32[]{:T(128)} %constant.54.clone.1..sunk.1) | dynamic-update-slice | bytes 917508 | tf_op jit(solution)/shard_map/while/body/jit(dynamic_update_index_in_dim)/dynamic_update_slice | solution.py:119
  413.3 4.2 fusion.123
  417.5 2.4 fusion.124
  420.6 2.7 bitcast_dynamic-update-slice_fusion.3
  425.9 2.3 fusion.125
  428.2 12.8 %dynamic_update_slice.26 = f32[4,896,128]{2,0,1:T(4,128)} dynamic-update-slice(f32[4,896,128]{2,0,1:T(4,128)} %get-tuple-element.368, f32[1,896,128]{2,0,1:T(1,128)S(1)} %bitcast.214, s32[]{:T(128)S(6)} %copy.88, s32[]{:T(128)} %constant.54.clone.1..sunk.1, s32[]{:T(128)} %constant.54.clone.1..sunk.1) | dynamic-update-slice | bytes 917508 | tf_op jit(solution)/shard_map/while/body/jit(dynamic_update_index_in_dim)/dynamic_update_slice | solution.py:119
  441.0 12.8 %dynamic_update_slice.27 = f32[4,896,128]{2,0,1:T(4,128)} dynamic-update-slice(f32[4,896,128]{2,0,1:T(4,128)} %get-tuple-element.369, f32[1,896,128]{2,0,1:T(1,128)S(1)} %bitcast.213, s32[]{:T(128)S(6)} %copy.88, s32[]{:T(128)} %constant.54.clone.1..sunk.1, s32[]{:T(128)} %constant.54.clone.1..sunk.1) | dynamic-update-slice | bytes 917508 | tf_op jit(solution)/shard_map/while/body/jit(dynamic_update_index_in_dim)/dynamic_update_slice | solution.py:119
  453.9 4.2 fusion.123
  458.2 2.4 fusion.124
  461.3 2.7 bitcast_dynamic-update-slice_fusion.3
  464.1 1.8 multiply_convert_fusion.2
  466.5 2.3 fusion.125
  468.9 12.8 %dynamic_update_slice.26 = f32[4,896,128]{2,0,1:T(4,128)} dynamic-update-slice(f32[4,896,128]{2,0,1:T(4,128)} %get-tuple-element.368, f32[1,896,128]{2,0,1:T(1,128)S(1)} %bitcast.214, s32[]{:T(128)S(6)} %copy.88, s32[]{:T(128)} %constant.54.clone.1..sunk.1, s32[]{:T(128)} %constant.54.clone.1..sunk.1) | dynamic-update-slice | bytes 917508 | tf_op jit(solution)/shard_map/while/body/jit(dynamic_update_index_in_dim)/dynamic_update_slice | solution.py:119
  481.7 12.8 %dynamic_update_slice.27 = f32[4,896,128]{2,0,1:T(4,128)} dynamic-update-slice(f32[4,896,128]{2,0,1:T(4,128)} %get-tuple-element.369, f32[1,896,128]{2,0,1:T(1,128)S(1)} %bitcast.213, s32[]{:T(128)S(6)} %copy.88, s32[]{:T(128)} %constant.54.clone.1..sunk.1, s32[]{:T(128)} %constant.54.clone.1..sunk.1) | dynamic-update-slice | bytes 917508 | tf_op jit(solution)/shard_map/while/body/jit(dynamic_update_index_in_dim)/dynamic_update_slice | solution.py:119
  494.4 2.8 copy.39
  498.4 1.9 collective-permute-start.12
  500.3 1.9 collective-permute-start.18
  502.3 2.9 copy.55
  505.1 2.0 collective-permute-done.12
  507.2 1.9 collective-permute-start.13
  510.5 1.9 collective-permute-start.19
  512.4 3.0 collective-permute-done.13
  515.5 1.9 collective-permute-start.14
  517.4 2.0 collective-permute-done.19
  519.5 1.9 collective-permute-start.20
  521.4 3.0 collective-permute-done.14
  524.5 1.9 collective-permute-start.15
  526.4 2.0 collective-permute-done.20
  528.5 1.9 collective-permute-start.21
  530.4 3.0 collective-permute-done.15
  533.5 1.9 collective-permute-start.16
  536.7 1.9 collective-permute-start.22
  538.6 3.0 collective-permute-done.16
  541.6 1.9 collective-permute-start.17
  544.8 1.9 collective-permute-start.23
  546.7 3.0 collective-permute-done.17
  550.4 2.4 collective-permute-done.23
  (173 shorter events, 80.8 us)
Async XLA Ops:
  0.6 307.2 %copy-start.3 = (bf16[128,32,128]{2,1,0:T(8,128)(2,1)S(1)}, bf16[128,32,128]{2,1,0:T(8,128)(2,1)}, u32[]{:S(2)}) copy-start(bf16[128,32,128]{2,1,0:T(8,128)(2,1)} %param.13) | copy-start | bytes 3145732
  1.8 8.2 %collective-permute-start.6 = (bf16[128,4,128]{0,2,1:T(8,128)(2,1)S(1)}, bf16[128,4,128]{0,2,1:T(8,128)(2,1)S(1)}, u32[]{:S(2)}, u32[]{:S(2)}) collective-permute-start(bf16[128,4,128]{0,2,1:T(8,128)(2,1)S(1)} %copy.34), channel_id=1, source_target_pairs={{0,1},{1,2},{2,3},{3,4},{4,5},{5,6},{6,7},{7,8},{8,9},{9,10},{10,1... | collective-permute-start | bytes 393224 | tf_op jit(solution)/shard_map/ppermute | solution.py:28
  7.4 7.4 %collective-permute-start = (bf16[128,4,128]{2,0,1:T(8,128)(2,1)S(1)}, bf16[128,4,128]{2,0,1:T(8,128)(2,1)S(1)}, u32[]{:S(2)}, u32[]{:S(2)}) collective-permute-start(bf16[128,4,128]{2,0,1:T(8,128)(2,1)S(1)} %copy.32), channel_id=1, source_target_pairs={{0,1},{1,2},{2,3},{3,4},{4,5},{5,6},{6,7},{7,8},{8,9},{9,10},{10,1... | collective-permute-start | bytes 393224 | tf_op jit(solution)/shard_map/ppermute | solution.py:28
  10.0 8.1 %collective-permute-start.7 = (bf16[128,4,128]{0,2,1:T(8,128)(2,1)S(1)}, bf16[128,4,128]{0,2,1:T(8,128)(2,1)S(1)}, u32[]{:S(2)}, u32[]{:S(2)}) collective-permute-start(bf16[128,4,128]{0,2,1:T(8,128)(2,1)S(1)} %collective-permute-done.6), channel_id=1, source_target_pairs={{0,1},{1,2},{2,3},{3,4},{4,5},{5,6},{6,7},{7,8},{8,9},{9,10},{10,1... | collective-permute-start | bytes 393224 | tf_op jit(solution)/shard_map/ppermute | solution.py:28
  14.8 8.8 %collective-permute-start.1 = (bf16[128,4,128]{2,0,1:T(8,128)(2,1)S(1)}, bf16[128,4,128]{2,0,1:T(8,128)(2,1)S(1)}, u32[]{:S(2)}, u32[]{:S(2)}) collective-permute-start(bf16[128,4,128]{2,0,1:T(8,128)(2,1)S(1)} %collective-permute-done), channel_id=1, source_target_pairs={{0,1},{1,2},{2,3},{3,4},{4,5},{5,6},{6,7},{7,8},{8,9},{9,10},{10,1... | collective-permute-start | bytes 393224 | tf_op jit(solution)/shard_map/ppermute | solution.py:28
  18.1 288.1 %copy-start.7 = (bf16[128,4,128]{0,2,1:T(8,128)(2,1)}, bf16[128,4,128]{0,2,1:T(8,128)(2,1)S(1)}, u32[]{:S(2)}) copy-start(bf16[128,4,128]{0,2,1:T(8,128)(2,1)S(1)} %collective-permute-done.7) | copy-start | bytes 393220
  18.1 8.9 %collective-permute-start.8 = (bf16[128,4,128]{0,2,1:T(8,128)(2,1)S(1)}, bf16[128,4,128]{0,2,1:T(8,128)(2,1)S(1)}, u32[]{:S(2)}, u32[]{:S(2)}) collective-permute-start(bf16[128,4,128]{0,2,1:T(8,128)(2,1)S(1)} %collective-permute-done.7), channel_id=1, source_target_pairs={{0,1},{1,2},{2,3},{3,4},{4,5},{5,6},{6,7},{7,8},{8,9},{9,10},{10,1... | collective-permute-start | bytes 393224 | tf_op jit(solution)/shard_map/ppermute | solution.py:28
  23.6 17.2 %copy-start.5 = (bf16[128,4,128]{2,0,1:T(8,128)(2,1)}, bf16[128,4,128]{2,0,1:T(8,128)(2,1)S(1)}, u32[]{:S(2)}) copy-start(bf16[128,4,128]{2,0,1:T(8,128)(2,1)S(1)} %collective-permute-done.1) | copy-start | bytes 393220
  23.6 9.7 %collective-permute-start.2 = (bf16[128,4,128]{2,0,1:T(8,128)(2,1)S(1)}, bf16[128,4,128]{2,0,1:T(8,128)(2,1)S(1)}, u32[]{:S(2)}, u32[]{:S(2)}) collective-permute-start(bf16[128,4,128]{2,0,1:T(8,128)(2,1)S(1)} %collective-permute-done.1), channel_id=1, source_target_pairs={{0,1},{1,2},{2,3},{3,4},{4,5},{5,6},{6,7},{7,8},{8,9},{9,10},{10,1... | collective-permute-start | bytes 393224 | tf_op jit(solution)/shard_map/ppermute | solution.py:28
  27.0 279.1 %copy-start.10 = (bf16[128,4,128]{0,2,1:T(8,128)(2,1)}, bf16[128,4,128]{0,2,1:T(8,128)(2,1)S(1)}, u32[]{:S(2)}) copy-start(bf16[128,4,128]{0,2,1:T(8,128)(2,1)S(1)} %collective-permute-done.8) | copy-start | bytes 393220
  27.0 8.3 %collective-permute-start.9 = (bf16[128,4,128]{0,2,1:T(8,128)(2,1)S(1)}, bf16[128,4,128]{0,2,1:T(8,128)(2,1)S(1)}, u32[]{:S(2)}, u32[]{:S(2)}) collective-permute-start(bf16[128,4,128]{0,2,1:T(8,128)(2,1)S(1)} %collective-permute-done.8), channel_id=1, source_target_pairs={{0,1},{1,2},{2,3},{3,4},{4,5},{5,6},{6,7},{7,8},{8,9},{9,10},{10,1... | collective-permute-start | bytes 393224 | tf_op jit(solution)/shard_map/ppermute | solution.py:28
  33.4 272.8 %copy-start.8 = (bf16[128,4,128]{2,0,1:T(8,128)(2,1)}, bf16[128,4,128]{2,0,1:T(8,128)(2,1)S(1)}, u32[]{:S(2)}) copy-start(bf16[128,4,128]{2,0,1:T(8,128)(2,1)S(1)} %collective-permute-done.2) | copy-start | bytes 393220
  33.4 259.9 %collective-permute-start.3 = (bf16[128,4,128]{2,0,1:T(8,128)(2,1)S(1)}, bf16[128,4,128]{2,0,1:T(8,128)(2,1)}, u32[]{:S(2)}, u32[]{:S(2)}) collective-permute-start(bf16[128,4,128]{2,0,1:T(8,128)(2,1)S(1)} %collective-permute-done.2), channel_id=1, source_target_pairs={{0,1},{1,2},{2,3},{3,4},{4,5},{5,6},{6,7},{7,8},{8,9},{9,10},{10,1... | collective-permute-start | bytes 393224 | tf_op jit(solution)/shard_map/ppermute | solution.py:28
  35.3 270.8 %copy-start.11 = (bf16[128,4,128]{0,2,1:T(8,128)(2,1)}, bf16[128,4,128]{0,2,1:T(8,128)(2,1)S(1)}, u32[]{:S(2)}) copy-start(bf16[128,4,128]{0,2,1:T(8,128)(2,1)S(1)} %collective-permute-done.9) | copy-start | bytes 393220
  35.3 265.0 %collective-permute-start.10 = (bf16[128,4,128]{0,2,1:T(8,128)(2,1)S(1)}, bf16[128,4,128]{0,2,1:T(8,128)(2,1)}, u32[]{:S(2)}, u32[]{:S(2)}) collective-permute-start(bf16[128,4,128]{0,2,1:T(8,128)(2,1)S(1)} %collective-permute-done.9), channel_id=1, source_target_pairs={{0,1},{1,2},{2,3},{3,4},{4,5},{5,6},{6,7},{7,8},{8,9},{9,10},{10,1... | collective-permute-start | bytes 393224 | tf_op jit(solution)/shard_map/ppermute | solution.py:28
  293.3 15.6 %collective-permute-start.4 = (bf16[128,4,128]{2,0,1:T(8,128)(2,1)}, bf16[128,4,128]{2,0,1:T(8,128)(2,1)}, u32[]{:S(2)}, u32[]{:S(2)}) collective-permute-start(bf16[128,4,128]{2,0,1:T(8,128)(2,1)} %collective-permute-done.3), channel_id=1, source_target_pairs={{0,1},{1,2},{2,3},{3,4},{4,5},{5,6},{6,7},{7,8},{8,9},{9,10},{10,1... | collective-permute-start | bytes 393224 | tf_op jit(solution)/shard_map/ppermute | solution.py:28
  300.4 19.3 %collective-permute-start.11 = (bf16[128,4,128]{0,2,1:T(8,128)(2,1)}, bf16[128,4,128]{0,2,1:T(8,128)(2,1)}, u32[]{:S(2)}, u32[]{:S(2)}) collective-permute-start(bf16[128,4,128]{0,2,1:T(8,128)(2,1)} %collective-permute-done.10), channel_id=1, source_target_pairs={{0,1},{1,2},{2,3},{3,4},{4,5},{5,6},{6,7},{7,8},{8,9},{9,10},{10,1... | collective-permute-start | bytes 393224 | tf_op jit(solution)/shard_map/ppermute | solution.py:28
  308.8 22.0 %copy-start.9 = (bf16[128,4,128]{2,0,1:T(8,128)(2,1)S(1)}, bf16[128,4,128]{2,0,1:T(8,128)(2,1)}, u32[]{:S(2)}) copy-start(bf16[128,4,128]{2,0,1:T(8,128)(2,1)} %copy-done.8) | copy-start | bytes 393220
  308.8 22.1 %copy-start.6 = (bf16[128,4,128]{2,0,1:T(8,128)(2,1)S(1)}, bf16[128,4,128]{2,0,1:T(8,128)(2,1)}, u32[]{:S(2)}) copy-start(bf16[128,4,128]{2,0,1:T(8,128)(2,1)} %copy-done.5) | copy-start | bytes 393220
  308.8 22.1 %copy-start.4 = (bf16[128,4,128]{2,1,0:T(4,128)(2,1)S(1)}, bf16[128,4,128]{2,1,0:T(4,128)(2,1)}, u32[]{:S(2)}) copy-start(bf16[128,4,128]{2,1,0:T(4,128)(2,1)} %param.10) | copy-start | bytes 393220
  308.9 20.1 %collective-permute-start.5 = (bf16[128,4,128]{2,0,1:T(8,128)(2,1)}, bf16[128,4,128]{2,0,1:T(8,128)(2,1)S(1)}, u32[]{:S(2)}, u32[]{:S(2)}) collective-permute-start(bf16[128,4,128]{2,0,1:T(8,128)(2,1)} %collective-permute-done.4), channel_id=1, source_target_pairs={{0,1},{1,2},{2,3},{3,4},{4,5},{5,6},{6,7},{7,8},{8,9},{9,10},{10,1... | collective-permute-start | bytes 393224 | tf_op jit(solution)/shard_map/ppermute | solution.py:28
  331.0 0.9 copy-start.12
  338.7 3.5 copy-start
  379.3 3.5 copy-start
  419.9 3.5 copy-start
  460.6 3.5 copy-start
  494.4 5.8 %copy-start.1 = (f32[4,896,128]{2,0,1:T(4,128)S(1)}, f32[4,896,128]{2,0,1:T(4,128)}, u32[]{:S(2)}) copy-start(f32[4,896,128]{2,0,1:T(4,128)} %get-tuple-element.98) | copy-start | bytes 5505028
  497.2 9.9 %copy-start.2 = (f32[4,896,128]{2,0,1:T(4,128)S(1)}, f32[4,896,128]{2,0,1:T(4,128)}, u32[]{:S(2)}) copy-start(f32[4,896,128]{2,0,1:T(4,128)} %get-tuple-element.97) | copy-start | bytes 5505028
  498.4 8.8 %collective-permute-start.12 = (bf16[128,4,128]{2,1,0:T(4,128)(2,1)S(1)}, bf16[128,4,128]{2,1,0:T(4,128)(2,1)S(1)}, u32[]{:S(2)}, u32[]{:S(2)}) collective-permute-start(bf16[128,4,128]{2,1,0:T(4,128)(2,1)S(1)} %fusion.81), channel_id=1, source_target_pairs={{1,0},{2,1},{3,2},{4,3},{5,4},{6,5},{7,6},{8,7},{9,8},{10,9},{11,1... | collective-permute-start | bytes 393224 | tf_op jit(solution)/shard_map/ppermute | solution.py:28
  500.3 10.1 %collective-permute-start.18 = (bf16[128,4,128]{2,1,0:T(4,128)(2,1)S(1)}, bf16[128,4,128]{2,1,0:T(4,128)(2,1)S(1)}, u32[]{:S(2)}, u32[]{:S(2)}) collective-permute-start(bf16[128,4,128]{2,1,0:T(4,128)(2,1)S(1)} %fusion.82), channel_id=1, source_target_pairs={{1,0},{2,1},{3,2},{4,3},{5,4},{6,5},{7,6},{8,7},{9,8},{10,9},{11,1... | collective-permute-start | bytes 393224 | tf_op jit(solution)/shard_map/ppermute | solution.py:28
  507.2 8.2 %collective-permute-start.13 = (bf16[128,4,128]{2,1,0:T(4,128)(2,1)S(1)}, bf16[128,4,128]{2,1,0:T(4,128)(2,1)S(1)}, u32[]{:S(2)}, u32[]{:S(2)}) collective-permute-start(bf16[128,4,128]{2,1,0:T(4,128)(2,1)S(1)} %fusion.80), channel_id=1, source_target_pairs={{1,0},{2,1},{3,2},{4,3},{5,4},{6,5},{7,6},{8,7},{9,8},{10,9},{11,1... | collective-permute-start | bytes 393224 | tf_op jit(solution)/shard_map/ppermute | solution.py:28
  510.5 8.9 %collective-permute-start.19 = (bf16[128,4,128]{2,1,0:T(4,128)(2,1)S(1)}, bf16[128,4,128]{2,1,0:T(4,128)(2,1)S(1)}, u32[]{:S(2)}, u32[]{:S(2)}) collective-permute-start(bf16[128,4,128]{2,1,0:T(4,128)(2,1)S(1)} %fusion.68), channel_id=1, source_target_pairs={{1,0},{2,1},{3,2},{4,3},{5,4},{6,5},{7,6},{8,7},{9,8},{10,9},{11,1... | collective-permute-start | bytes 393224 | tf_op jit(solution)/shard_map/ppermute | solution.py:28
  515.5 8.9 %collective-permute-start.14 = (bf16[128,4,128]{2,1,0:T(4,128)(2,1)S(1)}, bf16[128,4,128]{2,1,0:T(4,128)(2,1)S(1)}, u32[]{:S(2)}, u32[]{:S(2)}) collective-permute-start(bf16[128,4,128]{2,1,0:T(4,128)(2,1)S(1)} %fusion.78), channel_id=1, source_target_pairs={{1,0},{2,1},{3,2},{4,3},{5,4},{6,5},{7,6},{8,7},{9,8},{10,9},{11,1... | collective-permute-start | bytes 393224 | tf_op jit(solution)/shard_map/ppermute | solution.py:28
  519.5 8.9 %collective-permute-start.20 = (bf16[128,4,128]{2,1,0:T(4,128)(2,1)S(1)}, bf16[128,4,128]{2,1,0:T(4,128)(2,1)S(1)}, u32[]{:S(2)}, u32[]{:S(2)}) collective-permute-start(bf16[128,4,128]{2,1,0:T(4,128)(2,1)S(1)} %fusion.66), channel_id=1, source_target_pairs={{1,0},{2,1},{3,2},{4,3},{5,4},{6,5},{7,6},{8,7},{9,8},{10,9},{11,1... | collective-permute-start | bytes 393224 | tf_op jit(solution)/shard_map/ppermute | solution.py:28
  524.5 8.9 %collective-permute-start.15 = (bf16[128,4,128]{2,1,0:T(4,128)(2,1)S(1)}, bf16[128,4,128]{2,1,0:T(4,128)(2,1)S(1)}, u32[]{:S(2)}, u32[]{:S(2)}) collective-permute-start(bf16[128,4,128]{2,1,0:T(4,128)(2,1)S(1)} %fusion.76), channel_id=1, source_target_pairs={{1,0},{2,1},{3,2},{4,3},{5,4},{6,5},{7,6},{8,7},{9,8},{10,9},{11,1... | collective-permute-start | bytes 393224 | tf_op jit(solution)/shard_map/ppermute | solution.py:28
  528.5 8.1 %collective-permute-start.21 = (bf16[128,4,128]{2,1,0:T(4,128)(2,1)S(1)}, bf16[128,4,128]{2,1,0:T(4,128)(2,1)S(1)}, u32[]{:S(2)}, u32[]{:S(2)}) collective-permute-start(bf16[128,4,128]{2,1,0:T(4,128)(2,1)S(1)} %fusion.64), channel_id=1, source_target_pairs={{1,0},{2,1},{3,2},{4,3},{5,4},{6,5},{7,6},{8,7},{9,8},{10,9},{11,1... | collective-permute-start | bytes 393224 | tf_op jit(solution)/shard_map/ppermute | solution.py:28
  533.5 8.1 %collective-permute-start.16 = (bf16[128,4,128]{2,1,0:T(4,128)(2,1)S(1)}, bf16[128,4,128]{2,1,0:T(4,128)(2,1)S(1)}, u32[]{:S(2)}, u32[]{:S(2)}) collective-permute-start(bf16[128,4,128]{2,1,0:T(4,128)(2,1)S(1)} %fusion.74), channel_id=1, source_target_pairs={{1,0},{2,1},{3,2},{4,3},{5,4},{6,5},{7,6},{8,7},{9,8},{10,9},{11,1... | collective-permute-start | bytes 393224 | tf_op jit(solution)/shard_map/ppermute | solution.py:28
  536.7 8.1 %collective-permute-start.22 = (bf16[128,4,128]{2,1,0:T(4,128)(2,1)S(1)}, bf16[128,4,128]{2,1,0:T(4,128)(2,1)S(1)}, u32[]{:S(2)}, u32[]{:S(2)}) collective-permute-start(bf16[128,4,128]{2,1,0:T(4,128)(2,1)S(1)} %fusion.62), channel_id=1, source_target_pairs={{1,0},{2,1},{3,2},{4,3},{5,4},{6,5},{7,6},{8,7},{9,8},{10,9},{11,1... | collective-permute-start | bytes 393224 | tf_op jit(solution)/shard_map/ppermute | solution.py:28
  541.6 8.1 %collective-permute-start.17 = (bf16[128,4,128]{2,1,0:T(4,128)(2,1)S(1)}, bf16[128,4,128]{2,1,0:T(4,128)(2,1)S(1)}, u32[]{:S(2)}, u32[]{:S(2)}) collective-permute-start(bf16[128,4,128]{2,1,0:T(4,128)(2,1)S(1)} %fusion.72), channel_id=1, source_target_pairs={{1,0},{2,1},{3,2},{4,3},{5,4},{6,5},{7,6},{8,7},{9,8},{10,9},{11,1... | collective-permute-start | bytes 393224 | tf_op jit(solution)/shard_map/ppermute | solution.py:28
  544.8 8.1 %collective-permute-start.23 = (bf16[128,4,128]{2,1,0:T(4,128)(2,1)S(1)}, bf16[128,4,128]{2,1,0:T(4,128)(2,1)S(1)}, u32[]{:S(2)}, u32[]{:S(2)}) collective-permute-start(bf16[128,4,128]{2,1,0:T(4,128)(2,1)S(1)} %fusion.60), channel_id=1, source_target_pairs={{1,0},{2,1},{3,2},{4,3},{5,4},{6,5},{7,6},{8,7},{9,8},{10,9},{11,1... | collective-permute-start | bytes 393224 | tf_op jit(solution)/shard_map/ppermute | solution.py:28
where the time goes:
time: 560 us; the launch traced here: 554 us
  loops' own time  189 us (34%)
  local copies, waits for them, and re-layouts  170 us (30%)
  starting transfers between devices  82.2 us (15%)
  matrix products  49.5 us (9%)
  waiting for transfers between devices  27.8 us (5%)
  blocking collectives  19.6 us (4%)
  other arithmetic  14.6 us (3%)
    another operation x1, loops' own time, prefix(): return lax.fori_loop(0, place, one, state)  188 us
    dynamic_update_slice x8, local copies, waits for them, and re-layouts, shards(): lax.map(lambda member: head_terms(member, visible), (query_heads, key_hea...  102 us
    ppermute x24, starting transfers between devices, from_behind(): lax.ppermute(value, axis, [(source, source + steps) for source in range(i...  82.2 us
    dynamic_slice x59, local copies, waits for them, and re-layouts, one(): lax.dynamic_index_in_dim(a, turn, 0, False)  39.5 us
    ppermute x24, waiting for transfers between devices, from_behind(): lax.ppermute(value, axis, [(source, source + steps) for source in range(i...  27.8 us
    unnamed x45, local copies, waits for them, and re-layouts  20.3 us
    unnamed x1, blocking collectives  19.6 us
    sub x4, matrix products, head_terms(): shifted_exp = jnp.exp(scores - row_max)  16.9 us
  transfers between devices with their start and end apart: 24, of which 13 were waited for; matrix products, arithmetic and copies ran while one was open for 11% of the time, Pallas kernels for 0%

commit v1 on v0

v1 whole, which is shorter than its diff:
```python
import functools
import jax
import jax.numpy as jnp
from jax import lax
from jax.experimental import pallas as pl
from jax.experimental.pallas import tpu as pltpu
from jax.sharding import PartitionSpec as P
LOG2E = 1.4426950408889634
NB=7
ROWS=128; HD=128
NT=(((1,),(1,)),((),()))
TN=(((0,),(0,)),((),()))
NN=(((1,),(0,)),((),()))
def dot(a,b,d): return lax.dot_general(a,b,d,preferred_element_type=jnp.float32)

def kernel(q_ref, g_ref, own, b3, b6, u, v, att_ref, gq_ref, p0_ref, p3_ref, p6_ref, pu_ref, pv_ref,
           kw, vw, bias, pb, db, *, rc, scale):
    W=NB*ROWS
    n=8*ROWS+16
    def piece(k):
        return [(own,0),(u,0),(v,0),(b3,0),(u,n),(v,n),(b6,0)][k]
    hp=pl.program_id(0)
    @pl.when(hp==0)
    def _():
        segq=jnp.transpose(jnp.broadcast_to(own[8*ROWS:8*ROWS+1,:].astype(jnp.float32),(ROWS,ROWS)))
        for k in range(NB):
            r,o=piece(k)
            segk=jnp.broadcast_to(r[o+8*ROWS:o+8*ROWS+1,:].astype(jnp.float32),(ROWS,ROWS))
            vis=segk==segq
            if k==0:
                vis=vis & (lax.broadcasted_iota(jnp.int32,(ROWS,ROWS),1)<=lax.broadcasted_iota(jnp.int32,(ROWS,ROWS),0))
            bias[:, (6-k)*ROWS:(7-k)*ROWS]=jnp.where(vis,0.0,-1e30)
    for jj in range(2):
        for k in range(NB):
            r,o=piece(k)
            kw[(6-k)*ROWS:(7-k)*ROWS,:]=r[pl.ds(pl.multiple_of(o+(2*hp+jj)*ROWS,ROWS if o==0 else 16),ROWS),:]
            vw[(6-k)*ROWS:(7-k)*ROWS,:]=r[pl.ds(pl.multiple_of(o+(4+2*hp+jj)*ROWS,ROWS if o==0 else 16),ROWS),:]
        K=kw[...]; V=vw[...]
        tc=rc//8
        for c in range(8*ROWS//rc):
            ts=slice(c*tc,(c+1)*tc)
            qc=q_ref[ts,8*jj:8*jj+8,:].reshape(rc,HD)
            gc=g_ref[ts,8*jj:8*jj+8,:].reshape(rc,HD)
            s=dot(qc,K,NT).reshape(tc,8,W)*(scale*LOG2E)+bias[ts,:][:,None,:]
            s=s.reshape(rc,W)
            m=jnp.max(s,axis=-1,keepdims=True)
            e=jnp.exp2(s-m)
            l=jnp.sum(e,axis=-1,keepdims=True)
            p=e*(1.0/l)
            ph=p.astype(jnp.bfloat16)
            pb[c*rc:(c+1)*rc,:]=ph
            o=dot(ph,V,NN).astype(jnp.bfloat16)
            att_ref[ts,8*jj:8*jj+8,:]=o.reshape(tc,8,HD)
            delta=jnp.sum(gc.astype(jnp.float32)*o.astype(jnp.float32),axis=-1,keepdims=True)
            dp=dot(gc,V,NT)
            ds=(p*(dp-delta)).astype(jnp.bfloat16)
            db[c*rc:(c+1)*rc,:]=ds
            gq_ref[ts,8*jj:8*jj+8,:]=(dot(ds,K,NN)*scale).astype(jnp.bfloat16).reshape(tc,8,HD)
        Q=q_ref[:,8*jj:8*jj+8,:].reshape(8*ROWS,HD)
        G=g_ref[:,8*jj:8*jj+8,:].reshape(8*ROWS,HD)
        dk=dot(db[...],Q,TN)*scale
        dv=dot(pb[...],G,TN)
        for k in range(NB):
            dst,o=[(p0_ref,0),(pu_ref,0),(pv_ref,0),(p3_ref,0),(pu_ref,8*ROWS),(pv_ref,8*ROWS),(p6_ref,0)][k]
            sl=slice((6-k)*ROWS,(7-k)*ROWS)
            dst[pl.ds(pl.multiple_of(o+(2*hp+jj)*ROWS,ROWS),ROWS),:]=dk[sl].astype(dst.dtype)
            dst[pl.ds(pl.multiple_of(o+(4+2*hp+jj)*ROWS,ROWS),ROWS),:]=dv[sl].astype(dst.dtype)

def attn(q,g,own,b3,b6,u,v,rc=256):
    W=NB*ROWS
    hspec=pl.BlockSpec((ROWS,16,HD),lambda i:(0,i,0))
    full=lambda a: pl.BlockSpec(a.shape,lambda i:(0,)*len(a.shape))
    sd=jax.ShapeDtypeStruct
    outs=[sd(q.shape,jnp.bfloat16),sd(q.shape,jnp.bfloat16)]+[sd((8*ROWS,HD),jnp.float32)]*3+[sd((16*ROWS,HD),jnp.bfloat16)]*2
    return pl.pallas_call(functools.partial(kernel,rc=rc,scale=HD**-0.5),
        grid=(2,),
        in_specs=[hspec,hspec]+[full(x) for x in (own,b3,b6,u,v)],
        out_specs=[hspec,hspec]+[full(x) for x in outs[2:]],
        out_shape=outs,
        scratch_shapes=[pltpu.VMEM((W,HD),jnp.bfloat16),pltpu.VMEM((W,HD),jnp.bfloat16),pltpu.VMEM((ROWS,W),jnp.float32),
            pltpu.VMEM((8*ROWS,W),jnp.bfloat16),pltpu.VMEM((8*ROWS,W),jnp.bfloat16)],
        compiler_params=pltpu.CompilerParams(vmem_limit_bytes=48*2**20),
        name="attn",
    )(q,g,own,b3,b6,u,v)


def shift(value, steps):
    count = lax.axis_size("ctx")
    return lax.ppermute(value, "ctx", [(s, (s + steps) % count) for s in range(count)])


def shards(queries, keys, values, segment, grad_out):
    rows, groups, head = keys.shape
    n = 2 * groups * rows
    own = jnp.concatenate([
        jnp.transpose(keys, (1, 0, 2)).reshape(groups * rows, head),
        jnp.transpose(values, (1, 0, 2)).reshape(groups * rows, head),
        jnp.broadcast_to(segment.astype(jnp.bfloat16)[None, :], (16, rows)),
    ], 0)
    b3 = shift(own, 3)
    b6 = shift(own, 6)
    u = shift(jnp.concatenate([own, b3], 0), 1)
    v = shift(jnp.concatenate([b3, b6], 0), -1)
    att, gq, p0, p3, p6, pu, pv = attn(queries, grad_out, own, b3, b6, u, v)
    u = shift(pu, -1).astype(jnp.float32)
    v = shift(pv, 1).astype(jnp.float32)
    s3 = (p3 + u[n:] + v[:n]).astype(jnp.bfloat16)
    s6 = (p6 + v[n:]).astype(jnp.bfloat16)
    w = shift(s3, -3).astype(jnp.float32)
    z = shift(s6, -6).astype(jnp.float32)
    total = (p0 + u[:n] + w + z).astype(jnp.bfloat16).reshape(2, groups, rows, head)
    total = jnp.transpose(total, (0, 2, 1, 3))
    return att, gq, total[0], total[1]


def solution(mesh):
    part = P(("dp", "ctx"), None, None)
    return jax.shard_map(
        shards,
        mesh=mesh,
        in_specs=(part, part, part, P(("dp", "ctx")), part),
        out_specs=(part, part, part, part),
        check_vma=False,
    )
```

time: 560 us -> 120 us (0.21)
  the two profiles are of different devices: /device:TPU:478 before, /device:TPU:8 now
where the time goes in v1:
time: 120 us; the launch traced here: 119 us
  waiting for transfers between devices  51 us (42%)
  starting transfers between devices  41.9 us (35%)
  Pallas kernels  21.6 us (18%)
  local copies, waits for them, and re-layouts  2.86 us (2%)
    ppermute x8, waiting for transfers between devices, shift(): lax.ppermute(value, 'ctx', [(s, (s + steps) % count) for s in range(count)])  51 us
    ppermute x8, starting transfers between devices, shift(): lax.ppermute(value, 'ctx', [(s, (s + steps) % count) for s in range(count)])  41.9 us
    pallas_call x1, Pallas kernels, attn(): pl.pallas_call(functools.partial(kernel, rc=rc, scale=HD ** (-0.5)), grid...  21.6 us
  transfers between devices with their start and end apart: 8, of which 8 were waited for; matrix products, arithmetic and copies ran while one was open for 0% of the time, Pallas kernels for 0%

profile of v1, /device:TPU:8, one launch (start us, length us, event | category | flops | bytes accessed | tf_op | source)
XLA Modules:
  0.0 119.3 jit_solution(6211817769692940084)
XLA Ops:
  0.6 0.7 convert_element_type.24
  1.3 0.9 copy.9
  2.2 0.9 copy.10
  3.2 0.0 copy-start
  3.2 5.4 %collective-permute-start.1 = (bf16[1040,128]{1,0:T(8,128)(2,1)S(1)}, bf16[1040,128]{1,0:T(8,128)(2,1)S(1)}, u32[]{:S(2)}, u32[]{:S(2)}) collective-permute-start(bf16[1040,128]{1,0:T(8,128)(2,1)S(1)} %pad_maximum_fusion.2.own), channel_id=1, source_target_pairs={{0,6},{1,7},{2,8},{3,9},{4,10},{5,11},{6,12},{7,13},{8,14},{9,15},... | collective-permute-start | bytes 798728 | tf_op jit(solution)/shard_map/ppermute | solution.py:89
  8.6 5.5 %collective-permute-start = (bf16[1040,128]{1,0:T(8,128)(2,1)S(1)}, bf16[1040,128]{1,0:T(8,128)(2,1)S(1)}, u32[]{:S(2)}, u32[]{:S(2)}) collective-permute-start(bf16[1040,128]{1,0:T(8,128)(2,1)S(1)} %pad_maximum_fusion.2.own), channel_id=1, source_target_pairs={{0,3},{1,4},{2,5},{3,6},{4,7},{5,8},{6,9},{7,10},{8,11},{9,12},{10... | collective-permute-start | bytes 798728 | tf_op jit(solution)/shard_map/ppermute | solution.py:89
  14.1 9.8 %collective-permute-done.1.b6 = bf16[1040,128]{1,0:T(8,128)(2,1)S(1)} collective-permute-done((bf16[1040,128]{1,0:T(8,128)(2,1)S(1)}, bf16[1040,128]{1,0:T(8,128)(2,1)S(1)}, u32[]{:S(2)}, u32[]{:S(2)}) %collective-permute-start.1) | collective-permute-done | bytes 266272 | tf_op jit(solution)/shard_map/ppermute | solution.py:89
  24.0 11.1 %collective-permute-done.b3 = bf16[1040,128]{1,0:T(8,128)(2,1)S(1)} collective-permute-done((bf16[1040,128]{1,0:T(8,128)(2,1)S(1)}, bf16[1040,128]{1,0:T(8,128)(2,1)S(1)}, u32[]{:S(2)}, u32[]{:S(2)}) %collective-permute-start) | collective-permute-done | bytes 266272 | tf_op jit(solution)/shard_map/ppermute | solution.py:89
  35.0 0.1 pad_maximum_fusion.1
  35.1 4.8 %collective-permute-start.3 = (bf16[2080,128]{1,0:T(8,128)(2,1)S(1)}, bf16[2080,128]{1,0:T(8,128)(2,1)S(1)}, u32[]{:S(2)}, u32[]{:S(2)}) collective-permute-start(bf16[2080,128]{1,0:T(8,128)(2,1)S(1)} %get-tuple-element.20), channel_id=1, source_target_pairs={{0,63},{1,0},{2,1},{3,2},{4,3},{5,4},{6,5},{7,6},{8,7},{9,8},{10,9... | collective-permute-start | bytes 1597448 | tf_op jit(solution)/shard_map/ppermute | solution.py:89
  39.9 2.0 %collective-permute-start.2 = (bf16[2080,128]{1,0:T(8,128)(2,1)S(1)}, bf16[2080,128]{1,0:T(8,128)(2,1)S(1)}, u32[]{:S(2)}, u32[]{:S(2)}) collective-permute-start(bf16[2080,128]{1,0:T(8,128)(2,1)S(1)} %get-tuple-element.21), channel_id=1, source_target_pairs={{0,1},{1,2},{2,3},{3,4},{4,5},{5,6},{6,7},{7,8},{8,9},{9,10},{10,1... | collective-permute-start | bytes 1597448 | tf_op jit(solution)/shard_map/ppermute | solution.py:89
  42.0 8.2 %collective-permute-done.3.v = bf16[2080,128]{1,0:T(8,128)(2,1)S(1)} collective-permute-done((bf16[2080,128]{1,0:T(8,128)(2,1)S(1)}, bf16[2080,128]{1,0:T(8,128)(2,1)S(1)}, u32[]{:S(2)}, u32[]{:S(2)}) %collective-permute-start.3) | collective-permute-done | bytes 532512 | tf_op jit(solution)/shard_map/ppermute | solution.py:89
  50.2 3.7 %collective-permute-done.2.u = bf16[2080,128]{1,0:T(8,128)(2,1)S(1)} collective-permute-done((bf16[2080,128]{1,0:T(8,128)(2,1)S(1)}, bf16[2080,128]{1,0:T(8,128)(2,1)S(1)}, u32[]{:S(2)}, u32[]{:S(2)}) %collective-permute-start.2) | collective-permute-done | bytes 532512 | tf_op jit(solution)/shard_map/ppermute | solution.py:89
  53.9 0.0 copy-done
  53.9 21.6 %attn.1 = (bf16[128,32,128]{2,1,0:T(8,128)(2,1)}, bf16[128,32,128]{2,1,0:T(8,128)(2,1)}, f32[1024,128]{1,0:T(8,128)S(1)}, f32[1024,128]{1,0:T(8,128)S(1)}, f32[1...) custom-call(bf16[128,32,128]{2,1,0:T(8,128)(2,1)S(1)} %copy-done, ...), custom_call_target="tpu_custom_call" | custom-call | tf_op jit(solution)/shard_map/attn/pallas_call | solution.py:75
  75.5 6.5 %collective-permute-start.4 = (bf16[2048,128]{1,0:T(8,128)(2,1)S(1)}, bf16[2048,128]{1,0:T(8,128)(2,1)S(1)}, u32[]{:S(2)}, u32[]{:S(2)}) collective-permute-start(bf16[2048,128]{1,0:T(8,128)(2,1)S(1)} %get-tuple-element.14), channel_id=1, source_target_pairs={{0,63},{1,0},{2,1},{3,2},{4,3},{5,4},{6,5},{7,6},{8,7},{9,8},{10,9... | collective-permute-start | bytes 1572872 | tf_op jit(solution)/shard_map/ppermute | solution.py:89
  82.1 1.9 %collective-permute-start.5 = (bf16[2048,128]{1,0:T(8,128)(2,1)S(1)}, bf16[2048,128]{1,0:T(8,128)(2,1)S(1)}, u32[]{:S(2)}, u32[]{:S(2)}) collective-permute-start(bf16[2048,128]{1,0:T(8,128)(2,1)S(1)} %get-tuple-element.16), channel_id=1, source_target_pairs={{0,1},{1,2},{2,3},{3,4},{4,5},{5,6},{6,7},{7,8},{8,9},{9,10},{10,1... | collective-permute-start | bytes 1572872 | tf_op jit(solution)/shard_map/ppermute | solution.py:89
  84.0 6.1 %collective-permute-done.4 = bf16[2048,128]{1,0:T(8,128)(2,1)S(1)} collective-permute-done((bf16[2048,128]{1,0:T(8,128)(2,1)S(1)}, bf16[2048,128]{1,0:T(8,128)(2,1)S(1)}, u32[]{:S(2)}, u32[]{:S(2)}) %collective-permute-start.4) | collective-permute-done | bytes 524320 | tf_op jit(solution)/shard_map/ppermute | solution.py:89
  90.1 0.1 convert_element_type.25
  90.2 4.0 %collective-permute-done.5 = bf16[2048,128]{1,0:T(8,128)(2,1)S(1)} collective-permute-done((bf16[2048,128]{1,0:T(8,128)(2,1)S(1)}, bf16[2048,128]{1,0:T(8,128)(2,1)S(1)}, u32[]{:S(2)}, u32[]{:S(2)}) %collective-permute-start.5) | collective-permute-done | bytes 524320 | tf_op jit(solution)/shard_map/ppermute | solution.py:89
  94.2 0.1 convert_element_type.26
  94.3 0.1 fusion.1
  94.4 7.1 %collective-permute-start.6 = (bf16[1024,128]{1,0:T(8,128)(2,1)S(1)}, bf16[1024,128]{1,0:T(8,128)(2,1)S(1)}, u32[]{:S(2)}, u32[]{:S(2)}) collective-permute-start(bf16[1024,128]{1,0:T(8,128)(2,1)S(1)} %get-tuple-element.18), channel_id=1, source_target_pairs={{0,61},{1,62},{2,63},{3,0},{4,1},{5,2},{6,3},{7,4},{8,5},{9,6},{10... | collective-permute-start | bytes 786440 | tf_op jit(solution)/shard_map/ppermute | solution.py:89
  101.6 8.5 %collective-permute-start.7 = (bf16[1024,128]{1,0:T(8,128)(2,1)S(1)}, bf16[1024,128]{1,0:T(8,128)(2,1)S(1)}, u32[]{:S(2)}, u32[]{:S(2)}) collective-permute-start(bf16[1024,128]{1,0:T(8,128)(2,1)S(1)} %get-tuple-element.19), channel_id=1, source_target_pairs={{0,58},{1,59},{2,60},{3,61},{4,62},{5,63},{6,0},{7,1},{8,2},{9,3},... | collective-permute-start | bytes 786440 | tf_op jit(solution)/shard_map/ppermute | solution.py:89
  110.1 6.1 %collective-permute-done.6 = bf16[1024,128]{1,0:T(8,128)(2,1)S(1)} collective-permute-done((bf16[1024,128]{1,0:T(8,128)(2,1)S(1)}, bf16[1024,128]{1,0:T(8,128)(2,1)S(1)}, u32[]{:S(2)}, u32[]{:S(2)}) %collective-permute-start.6) | collective-permute-done | bytes 262176 | tf_op jit(solution)/shard_map/ppermute | solution.py:89
  116.2 2.0 %collective-permute-done.7 = bf16[1024,128]{1,0:T(8,128)(2,1)S(1)} collective-permute-done((bf16[1024,128]{1,0:T(8,128)(2,1)S(1)}, bf16[1024,128]{1,0:T(8,128)(2,1)S(1)}, u32[]{:S(2)}, u32[]{:S(2)}) %collective-permute-start.7) | collective-permute-done | bytes 262176 | tf_op jit(solution)/shard_map/ppermute | solution.py:89
  118.2 0.1 fusion.4
  118.3 0.2 copy.13
  118.5 0.8 slice_bitcast_fusion
  (2 shorter events, 0.0 us)
Async XLA Ops:
  3.2 50.7 %copy-start = (bf16[128,32,128]{2,1,0:T(8,128)(2,1)S(1)}, bf16[128,32,128]{2,1,0:T(8,128)(2,1)}, u32[]{:S(2)}) copy-start(bf16[128,32,128]{2,1,0:T(8,128)(2,1)} %q_ref.1) | copy-start | bytes 3145732
  3.2 20.8 %collective-permute-start.1 = (bf16[1040,128]{1,0:T(8,128)(2,1)S(1)}, bf16[1040,128]{1,0:T(8,128)(2,1)S(1)}, u32[]{:S(2)}, u32[]{:S(2)}) collective-permute-start(bf16[1040,128]{1,0:T(8,128)(2,1)S(1)} %pad_maximum_fusion.2.own), channel_id=1, source_target_pairs={{0,6},{1,7},{2,8},{3,9},{4,10},{5,11},{6,12},{7,13},{8,14},{9,15},... | collective-permute-start | bytes 798728 | tf_op jit(solution)/shard_map/ppermute | solution.py:89
  8.6 26.4 %collective-permute-start = (bf16[1040,128]{1,0:T(8,128)(2,1)S(1)}, bf16[1040,128]{1,0:T(8,128)(2,1)S(1)}, u32[]{:S(2)}, u32[]{:S(2)}) collective-permute-start(bf16[1040,128]{1,0:T(8,128)(2,1)S(1)} %pad_maximum_fusion.2.own), channel_id=1, source_target_pairs={{0,3},{1,4},{2,5},{3,6},{4,7},{5,8},{6,9},{7,10},{8,11},{9,12},{10... | collective-permute-start | bytes 798728 | tf_op jit(solution)/shard_map/ppermute | solution.py:89
  35.1 15.1 %collective-permute-start.3 = (bf16[2080,128]{1,0:T(8,128)(2,1)S(1)}, bf16[2080,128]{1,0:T(8,128)(2,1)S(1)}, u32[]{:S(2)}, u32[]{:S(2)}) collective-permute-start(bf16[2080,128]{1,0:T(8,128)(2,1)S(1)} %get-tuple-element.20), channel_id=1, source_target_pairs={{0,63},{1,0},{2,1},{3,2},{4,3},{5,4},{6,5},{7,6},{8,7},{9,8},{10,9... | collective-permute-start | bytes 1597448 | tf_op jit(solution)/shard_map/ppermute | solution.py:89
  39.9 13.9 %collective-permute-start.2 = (bf16[2080,128]{1,0:T(8,128)(2,1)S(1)}, bf16[2080,128]{1,0:T(8,128)(2,1)S(1)}, u32[]{:S(2)}, u32[]{:S(2)}) collective-permute-start(bf16[2080,128]{1,0:T(8,128)(2,1)S(1)} %get-tuple-element.21), channel_id=1, source_target_pairs={{0,1},{1,2},{2,3},{3,4},{4,5},{5,6},{6,7},{7,8},{8,9},{9,10},{10,1... | collective-permute-start | bytes 1597448 | tf_op jit(solution)/shard_map/ppermute | solution.py:89
  75.5 14.6 %collective-permute-start.4 = (bf16[2048,128]{1,0:T(8,128)(2,1)S(1)}, bf16[2048,128]{1,0:T(8,128)(2,1)S(1)}, u32[]{:S(2)}, u32[]{:S(2)}) collective-permute-start(bf16[2048,128]{1,0:T(8,128)(2,1)S(1)} %get-tuple-element.14), channel_id=1, source_target_pairs={{0,63},{1,0},{2,1},{3,2},{4,3},{5,4},{6,5},{7,6},{8,7},{9,8},{10,9... | collective-permute-start | bytes 1572872 | tf_op jit(solution)/shard_map/ppermute | solution.py:89
  82.1 12.2 %collective-permute-start.5 = (bf16[2048,128]{1,0:T(8,128)(2,1)S(1)}, bf16[2048,128]{1,0:T(8,128)(2,1)S(1)}, u32[]{:S(2)}, u32[]{:S(2)}) collective-permute-start(bf16[2048,128]{1,0:T(8,128)(2,1)S(1)} %get-tuple-element.16), channel_id=1, source_target_pairs={{0,1},{1,2},{2,3},{3,4},{4,5},{5,6},{6,7},{7,8},{8,9},{9,10},{10,1... | collective-permute-start | bytes 1572872 | tf_op jit(solution)/shard_map/ppermute | solution.py:89
  94.4 21.7 %collective-permute-start.6 = (bf16[1024,128]{1,0:T(8,128)(2,1)S(1)}, bf16[1024,128]{1,0:T(8,128)(2,1)S(1)}, u32[]{:S(2)}, u32[]{:S(2)}) collective-permute-start(bf16[1024,128]{1,0:T(8,128)(2,1)S(1)} %get-tuple-element.18), channel_id=1, source_target_pairs={{0,61},{1,62},{2,63},{3,0},{4,1},{5,2},{6,3},{7,4},{8,5},{9,6},{10... | collective-permute-start | bytes 786440 | tf_op jit(solution)/shard_map/ppermute | solution.py:89
  101.6 16.6 %collective-permute-start.7 = (bf16[1024,128]{1,0:T(8,128)(2,1)S(1)}, bf16[1024,128]{1,0:T(8,128)(2,1)S(1)}, u32[]{:S(2)}, u32[]{:S(2)}) collective-permute-start(bf16[1024,128]{1,0:T(8,128)(2,1)S(1)} %get-tuple-element.19), channel_id=1, source_target_pairs={{0,58},{1,59},{2,60},{3,61},{4,62},{5,63},{6,0},{7,1},{8,2},{9,3},... | collective-permute-start | bytes 786440 | tf_op jit(solution)/shard_map/ppermute | solution.py:89
